TPU v7x, 32 devices: a whole 2x2x4 slice. The times are simulated.
32 devices in a mesh: groups: 2 (over y), ep: 8 (over z, core), rep: 2 (over x).
Axes of the slice: x: 2, y: 2, z: 4, core: 2. Of those that a mesh axis runs over, the one named last changes fastest.
Arguments:
- tokens: bfloat16 [1024, 2048], P(('groups', 'ep')), parts along dimension 0, may hold values from -6 to 6
- choices: int32 [1024, 8], P(('groups', 'ep')), parts along dimension 0, may hold values from 0 to 15, all different within a row; in each aligned block of 64 rows (0 to 63, 64 to 127, ...) at most 64 rows name the same one
- route_weight: float32 [1024, 8], P(('groups', 'ep')), parts along dimension 0, may hold values from 0.05 to 0.3
- gate_proj: bfloat16 [16, 2048, 768], P('ep', None, 'rep'), may hold values from -0.125 to 0.125
- up_proj: bfloat16 [16, 2048, 768], P('ep', None, 'rep'), may hold values from -0.125 to 0.125
- down_proj: bfloat16 [16, 768, 2048], P('ep', 'rep'), may hold values from -0.21875 to 0.21875
Outputs:
- mixed: bfloat16 [1024, 2048], P(('groups', 'ep'), 'rep'), parts along dimension 0
There are 2 independent parts, one for each index of `groups`. A program takes and returns all parts, laid end to end along the dimension named above; an argument that names none is the same for every part. Nothing has to cross between parts.
Inputs may be any that keep to these rules, and one draw needn't show every extreme that they name: `choices`: each row names 8 different experts. In each aligned block of 64 rows no expert is named by more than 64 rows, a bound that some block reaches.
All inputs are finite; a program needn't handle non-finite values.
Results may differ from a plain program's by a relative error of at most 0.0085.
Values may be sent and summed in bfloat16 or wider, within the bound.
A program may use at most 64 MiB of HBM per device.

v0:
```python
import jax
import jax.numpy as jnp
from jax import lax
from jax.sharding import PartitionSpec as P


def local(tokens, choices, route_weight, gate_proj, up_proj, down_proj):
    n_ep = lax.axis_size("ep")
    n_rep = lax.axis_size("rep")
    exp_dev = gate_proj.shape[0]
    num_experts = exp_dev * n_ep
    tok_rows = tokens.shape[0]
    picks = choices.shape[1]
    width = tokens.shape[1]
    slot_cap = min(tok_rows, (2 * tok_rows * picks // num_experts + n_rep - 1) // n_rep * n_rep)
    slot_total = num_experts * slot_cap
    flat_choice = choices.reshape(-1)
    expert_ids = jnp.arange(num_experts, dtype=jnp.int32)
    onehot = (flat_choice[:, None] == expert_ids[None, :]).astype(jnp.int32)
    before = jnp.cumsum(onehot, axis=0) - onehot
    rank = jnp.sum(before * onehot, axis=1)
    slot_ids = flat_choice * slot_cap + rank
    all_slots = jnp.arange(slot_total, dtype=jnp.int32)
    select = (slot_ids[:, None] == all_slots[None, :]).reshape(tok_rows, picks, slot_total)
    dispatch = jnp.sum(select.astype(jnp.bfloat16), axis=1)
    combine = jnp.sum(jnp.where(select, route_weight[:, :, None], 0.0), axis=1)
    combine_high = combine.astype(jnp.bfloat16)
    combine_low = (combine - combine_high.astype(jnp.float32)).astype(jnp.bfloat16)
    buffer = jnp.einsum("ts,td->sd", dispatch, tokens, preferred_element_type=jnp.float32)
    buffer = buffer.astype(jnp.bfloat16).reshape(n_ep, exp_dev, slot_cap, width)
    arrived = lax.all_to_all(buffer, "ep", split_axis=0, concat_axis=0, tiled=True)
    gate_val = jnp.einsum("sjcd,jdh->sjch", arrived, gate_proj, preferred_element_type=jnp.float32)
    up_val = jnp.einsum("sjcd,jdh->sjch", arrived, up_proj, preferred_element_type=jnp.float32)
    hidden = (jax.nn.silu(gate_val) * up_val).astype(jnp.bfloat16)
    partial_out = jnp.einsum(
        "sjch,jhd->sjcd", hidden, down_proj, preferred_element_type=jnp.float32
    )
    expert_out = lax.psum_scatter(
        partial_out.astype(jnp.bfloat16), "rep", scatter_dimension=3, tiled=True
    )
    returned = lax.all_to_all(expert_out, "ep", split_axis=0, concat_axis=0, tiled=True)
    returned_rows = returned.reshape(slot_total, -1)
    mixed = jnp.dot(combine_high, returned_rows, preferred_element_type=jnp.float32)
    mixed = mixed + jnp.dot(combine_low, returned_rows, preferred_element_type=jnp.float32)
    return mixed.astype(jnp.bfloat16)


def solution(mesh):
    placed = (
        P(("groups", "ep"), None),
        P(("groups", "ep"), None),
        P(("groups", "ep"), None),
        P("ep", None, "rep"),
        P("ep", None, "rep"),
        P("ep", "rep", None),
    )
    return jax.shard_map(
        local, mesh=mesh, in_specs=placed, out_specs=P(("groups", "ep"), "rep"), check_vma=False
    )
```

profile of v0, /device:TPU:0, one launch (start us, length us, event | category | flops | bytes accessed | tf_op | source)
XLA Modules:
  0.0 249.3 jit_solution(14430175307891705766)
XLA Ops:
  6.5 0.0 copy-start
  6.5 0.0 reduce-scatter.2.cloned.1.call-start
  6.5 0.9 copy.36
  7.5 0.1 eq.43
  7.6 0.1 eq.39
  7.7 1.2 reduce-window.6
  8.8 0.2 slice_reduce_fusion
  9.1 0.1 fusion.28
  9.2 0.1 reduce_sum.33
  9.3 0.1 copy.39
  9.3 0.7 multiply_add_fusion
  10.0 0.1 copy.40
  10.1 0.7 fusion.21
  10.8 2.2 convolution_convert_fusion
  13.0 0.0 copy-start.3
  13.1 100.4 %all_to_all.10 = bf16[8,2,64,2048]{3,2,1,0:T(8,128)(2,1)S(1)} all-to-all(bf16[8,2,64,2048]{3,2,1,0:T(8,128)(2,1)S(1)} %bitcast.67), channel_id=1, replica_groups=mesh['groups'=2,'ep'=8,'rep'=2] {'ep'}, dimensions={0} | all-to-all | bytes 8388608 | tf_op jit(solution)/shard_map/all_to_all | solution.py:31
  113.5 2.0 copy-done.1
  115.4 0.0 copy-done.3
  115.4 3.6 %fusion.2 = f32[2,8,64,384]{3,2,1,0:T(8,128)} fusion(bf16[8,2,64,2048]{3,2,1,0:T(8,128)(2,1)S(1)} %all_to_all.10, bf16[2,2048,384]{2,1,0:T(8,128)(2,1)S(1)} %copy-done.3), kind=kOutput, calls=%fused_computation.4 | convolution fusion | flops 1610612736 | bytes 8912896 | tf_op jit(solution)/shard_map/sjcd,jdh->sjch/dot_general | solution.py:32
  119.0 0.0 copy-done
  119.0 8.2 %convert_bitcast_fusion = bf16[8,2,64,2048]{3,2,0,1:T(8,128)(2,1)} fusion(bf16[2,384,2048]{2,1,0:T(8,128)(2,1)S(1)} %copy-done, f32[2,8,64,384]{3,2,1,0:T(8,128)} %fusion.2, bf16[2,2048,384]{2,1,0:T(8,128)(2,1)} %param.10, bf16[8,2,64,2048]{3,2,1,0:T(8,128)(2,1)} %copy-done.1), kind=kOutput, calls=%fused_computation | convolution fusion | flops 3225681920 | bytes 16252928 | tf_op jit(solution)/shard_map/sjch,jhd->sjcd/dot_general | solution.py:35
  127.2 0.0 reduce-scatter.2.cloned.1.call-update
  127.3 53.3 %reduce-scatter.2.cloned.1.call-done = bf16[8,2,64,1024]{3,2,0,1:T(8,128)(2,1)} async-done(((bf16[8,2,64,2048]{3,2,0,1:T(8,128)(2,1)}), bf16[8,2,64,1024]{3,2,0,1:T(8,128)(2,1)}) %reduce-scatter.2.cloned.1.call-update) | async-done | bytes 2097168 | tf_op jit(solution)/shard_map/reduce_scatter | solution.py:38
  180.6 3.2 %copy.44 = bf16[8,2,64,1024]{3,2,1,0:T(8,128)(2,1)} copy(bf16[8,2,64,1024]{3,2,0,1:T(8,128)(2,1)} %reduce-scatter.2.cloned.1.call-done) | data formatting | bytes 4194304 | tf_op jit(solution)/shard_map/reduce_scatter | solution.py:38
  183.8 0.0 copy-start.2
  183.8 4.7 %all-to-all-start.1 = ((bf16[8,2,64,1024]{3,2,1,0:T(8,128)(2,1)}), bf16[8,2,64,1024]{3,2,1,0:T(8,128)(2,1)}, u32[]{:S(2)}, u32[]{:S(2)}) async-start(bf16[8,2,64,1024]{3,2,1,0:T(8,128)(2,1)} %copy.44), calls=%async_computation.2 | async-start | bytes 4194304 | tf_op jit(solution)/shard_map/all_to_all | solution.py:41
  188.5 0.0 copy-done.2
  188.5 0.1 copy.41
  188.6 0.7 select_reduce_fusion
  189.3 48.4 %all-to-all-done.1 = bf16[8,2,64,1024]{3,2,1,0:T(8,128)(2,1)} async-done(((bf16[8,2,64,1024]{3,2,1,0:T(8,128)(2,1)}), bf16[8,2,64,1024]{3,2,1,0:T(8,128)(2,1)}, u32[]{:S(2)}, u32[]{:S(2)}) %all-to-all-start.1) | async-done | bytes 2097184 | tf_op jit(solution)/shard_map/all_to_all | solution.py:41
  237.7 2.1 fusion.24
  239.8 2.7 %fusion.20 = bf16[64,1024]{1,0:T(8,128)(2,1)} fusion(f32[64,1024]{1,0:T(8,128)S(1)} %fusion.24, bf16[1024,1024]{1,0:T(8,128)(2,1)} %bitcast.11, f32[64,1024]{1,0:T(8,128)S(1)} %select_reduce_fusion), kind=kOutput, calls=%fused_computation.20 | convolution fusion | flops 134610944 | bytes 2752512 | tf_op jit(solution)/shard_map/dot_general | solution.py:44
  (4 shorter events, 0.0 us)
Async XLA Ops:
  6.5 112.5 %copy-start = (bf16[2,384,2048]{2,1,0:T(8,128)(2,1)S(1)}, bf16[2,384,2048]{2,1,0:T(8,128)(2,1)}, u32[]{:S(2)}) copy-start(bf16[2,384,2048]{2,1,0:T(8,128)(2,1)} %param.11) | copy-start | bytes 9437188
  6.5 174.1 %reduce-scatter.2.cloned.1.call-start = ((), (), s32[]{:S(2)}) async-start(), calls=%async_computation.3 | async-start | bytes 6291456 | tf_op jit(solution)/shard_map/reduce_scatter | solution.py:38
  13.0 102.4 %copy-start.3 = (bf16[2,2048,384]{2,1,0:T(8,128)(2,1)S(1)}, bf16[2,2048,384]{2,1,0:T(8,128)(2,1)}, u32[]{:S(2)}) copy-start(bf16[2,2048,384]{2,1,0:T(8,128)(2,1)} %param.9) | copy-start | bytes 9437188
  113.5 2.0 copy-start.1
  183.8 4.8 %copy-start.2 = (f32[64,8]{0,1:T(8,128)S(1)}, f32[64,8]{0,1:T(8,128)}, u32[]{:S(2)}) copy-start(f32[64,8]{0,1:T(8,128)} %param.8) | copy-start | bytes 6148
  183.8 53.9 %all-to-all-start.1 = ((bf16[8,2,64,1024]{3,2,1,0:T(8,128)(2,1)}), bf16[8,2,64,1024]{3,2,1,0:T(8,128)(2,1)}, u32[]{:S(2)}, u32[]{:S(2)}) async-start(bf16[8,2,64,1024]{3,2,1,0:T(8,128)(2,1)} %copy.44), calls=%async_computation.2 | async-start | bytes 4194304 | tf_op jit(solution)/shard_map/all_to_all | solution.py:41
Sparse Core Ops, SparseCore 0:
  127.4 53.1 reduce-scatter.1
where the time goes:
time: 250 us; the launch traced here: 249 us
  waiting for transfers between devices  102 us (41%)
  blocking collectives  100 us (40%)
  matrix products  18.8 us (8%)
  between operations  13.5 us (5%)
  local copies, waits for them, and re-layouts  6.8 us (3%)
  starting transfers between devices  4.75 us (2%)
  other arithmetic  3.39 us (1%)
    all_to_all x1, blocking collectives, local(): lax.all_to_all(buffer, 'ep', split_axis=0, concat_axis=0, tiled=True)  100 us
    reduce_scatter x1, waiting for transfers between devices, local(): lax.psum_scatter(partial_out.astype(jnp.bfloat16), 'rep', scatter_dimensi...  53.3 us
    all_to_all x1, waiting for transfers between devices, local(): lax.all_to_all(expert_out, 'ep', split_axis=0, concat_axis=0, tiled=True)  48.4 us
    dot_general x1, matrix products, local(): jnp.einsum('sjch,jhd->sjcd', hidden, down_proj, preferred_element_type=jn...  8.24 us
  transfers between devices with their start and end apart: 2, of which 2 were waited for; matrix products, arithmetic and copies ran while one was open for 0% of the time, Pallas kernels for 0%

commit v1 on v0

--- a/solution.py
+++ b/solution.py
@@ -2,6 +2,17 @@
 import jax.numpy as jnp
 from jax import lax
 from jax.sharding import PartitionSpec as P
+
+
+def split_up(x, dim, size):
+    before, after = (x.shape[:dim], x.shape[dim + 1 :])
+    return jnp.moveaxis(x.reshape(*before, size, -1, *after), dim, 0)
+
+
+def laid_out(blocks, dim):
+    shape = list(blocks.shape[1:])
+    shape[dim] *= blocks.shape[0]
+    return jnp.moveaxis(blocks, 0, dim).reshape(shape)
 
 
 def local(tokens, choices, route_weight, gate_proj, up_proj, down_proj):
@@ -38,7 +49,14 @@
     expert_out = lax.psum_scatter(
         partial_out.astype(jnp.bfloat16), "rep", scatter_dimension=3, tiled=True
     )
-    returned = lax.all_to_all(expert_out, "ep", split_axis=0, concat_axis=0, tiled=True)
+    size, index = (lax.axis_size("ep"), lax.axis_index("ep"))
+    blocks = split_up(expert_out, 0, size)
+    finished = [blocks[index]]
+    for lap in range(1, size):
+        sent = blocks[index ^ lap]
+        finished.append(lax.ppermute(sent, "ep", [(i, i ^ lap) for i in range(size)]))
+    blocks = jnp.stack(finished)[index ^ jnp.arange(size)]
+    returned = laid_out(blocks, 0)
     returned_rows = returned.reshape(slot_total, -1)
     mixed = jnp.dot(combine_high, returned_rows, preferred_element_type=jnp.float32)
     mixed = mixed + jnp.dot(combine_low, returned_rows, preferred_element_type=jnp.float32)

time: 250 us -> 247 us (0.988)
  the two profiles are of different devices: /device:TPU:0 before, /device:TPU:17 now
where the time goes in v1:
time: 247 us
  blocking collectives  95.7 us (39%)
  waiting for transfers between devices  92.7 us (38%)
  matrix products  17.4 us (7%)
  local copies, waits for them, and re-layouts  16.2 us (7%)
  between operations  13.5 us (5%)
  starting transfers between devices  7.72 us (3%)
  other arithmetic  3.41 us (1%)
    all_to_all x1, blocking collectives, local(): lax.all_to_all(buffer, 'ep', split_axis=0, concat_axis=0, tiled=True)  95.7 us
    reduce_scatter x1, waiting for transfers between devices, local(): lax.psum_scatter(partial_out.astype(jnp.bfloat16), 'rep', scatter_dimensi...  55.6 us
    ppermute x7, waiting for transfers between devices, local(): lax.ppermute(sent, 'ep', [(i, i ^ lap) for i in range(size)])  37 us
    unnamed x19, local copies, waits for them, and re-layouts  9.63 us
    dot_general x1, matrix products, local(): jnp.einsum('sjch,jhd->sjcd', hidden, down_proj, preferred_element_type=jn...  8.24 us
    ppermute x7, starting transfers between devices, local(): lax.ppermute(sent, 'ep', [(i, i ^ lap) for i in range(size)])  7.72 us
  transfers between devices with their start and end apart: 8, of which 6 were waited for; matrix products, arithmetic and copies ran while one was open for 3% of the time, Pallas kernels for 0%

profile of v1, /device:TPU:17, one launch (start us, length us, event | category | flops | bytes accessed | tf_op | source)
XLA Modules:
  0.0 246.6 jit_solution(8498548859810654235)
XLA Ops:
  6.5 0.9 copy.57
  7.7 1.2 reduce-window.6
  9.3 0.7 multiply_add_fusion
  10.1 0.7 fusion.21
  10.8 2.2 convolution_convert_fusion
  13.0 95.7 %all_to_all.5 = bf16[8,2,64,2048]{3,2,1,0:T(8,128)(2,1)S(1)} all-to-all(bf16[8,2,64,2048]{3,2,1,0:T(8,128)(2,1)S(1)} %bitcast.100), channel_id=1, replica_groups=mesh['groups'=2,'ep'=8,'rep'=2] {'ep'}, dimensions={0} | all-to-all | bytes 8388608 | tf_op jit(solution)/shard_map/all_to_all | solution.py:42
  108.8 2.0 copy-done.2
  110.8 3.6 %fusion.2 = f32[2,8,64,384]{3,2,1,0:T(8,128)} fusion(bf16[8,2,64,2048]{3,2,1,0:T(8,128)(2,1)S(1)} %all_to_all.5, bf16[2,2048,384]{2,1,0:T(8,128)(2,1)S(1)} %copy-done.4), kind=kOutput, calls=%fused_computation.5 | convolution fusion | flops 1610612736 | bytes 8912896 | tf_op jit(solution)/shard_map/sjcd,jdh->sjch/dot_general | solution.py:43
  114.3 8.2 %convert_bitcast_fusion = bf16[8,2,64,2048]{3,2,0,1:T(8,128)(2,1)} fusion(bf16[2,384,2048]{2,1,0:T(8,128)(2,1)S(1)} %copy-done, f32[2,8,64,384]{3,2,1,0:T(8,128)} %fusion.2, bf16[2,2048,384]{2,1,0:T(8,128)(2,1)} %param.10, bf16[8,2,64,2048]{3,2,1,0:T(8,128)(2,1)} %copy-done.2), kind=kOutput, calls=%fused_computation.1 | convolution fusion | flops 3225681920 | bytes 16252928 | tf_op jit(solution)/shard_map/sjch,jhd->sjcd/dot_general | solution.py:46
  123.3 55.6 %reduce-scatter.2.cloned.1.call-done = bf16[8,2,64,1024]{3,2,0,1:T(8,128)(2,1)} async-done(((bf16[8,2,64,2048]{3,2,0,1:T(8,128)(2,1)}), bf16[8,2,64,1024]{3,2,0,1:T(8,128)(2,1)}) %reduce-scatter.2.cloned.1.call-update) | async-done | bytes 2097168 | tf_op jit(solution)/shard_map/reduce_scatter | solution.py:49
  179.0 1.6 constant_dynamic-slice_fusion
  180.6 0.7 collective-permute-start
  181.3 0.7 select_reduce_fusion
  182.1 1.3 collective-permute-start.1
  184.0 2.5 %collective-permute-start.4 = (bf16[1,2,64,1024]{3,2,1,0:T(8,128)(2,1)S(1)}, bf16[1,2,64,1024]{3,2,1,0:T(8,128)(2,1)S(1)}, u32[]{:S(2)}, u32[]{:S(2)}) collective-permute-start(bf16[1,2,64,1024]{3,2,1,0:T(8,128)(2,1)S(1)} %get-tuple-element.6), channel_id=1, source_target_pairs={{0,10},{2,8},{4,14},{6,12},{8,2},{10,0},{12,6},{14,4},{1,11},{3,9}... | collective-permute-start | bytes 786440 | tf_op jit(solution)/shard_map/ppermute | solution.py:57
  186.5 1.7 bitcast_dynamic-update-slice_fusion.7
  188.5 0.7 bitcast_dynamic-update-slice_fusion.6
  189.2 8.6 %collective-permute-done.1 = bf16[1,2,64,1024]{3,2,1,0:T(8,128)(2,1)S(1)} collective-permute-done((bf16[1,2,64,1024]{3,2,1,0:T(8,128)(2,1)S(1)}, bf16[1,2,64,1024]{3,2,1,0:T(8,128)(2,1)S(1)}, u32[]{:S(2)}, u32[]{:S(2)}) %collective-permute-start.1) | collective-permute-done | bytes 262176 | tf_op jit(solution)/shard_map/ppermute | solution.py:57
  197.8 2.3 collective-permute-start.6
  200.0 0.7 bitcast_dynamic-update-slice_fusion.5
  200.8 2.6 %collective-permute-done.2 = bf16[1,2,64,1024]{3,2,1,0:T(8,128)(2,1)S(1)} collective-permute-done((bf16[1,2,64,1024]{3,2,1,0:T(8,128)(2,1)S(1)}, bf16[1,2,64,1024]{3,2,1,0:T(8,128)(2,1)S(1)}, u32[]{:S(2)}, u32[]{:S(2)}) %collective-permute-start.2) | collective-permute-done | bytes 262176 | tf_op jit(solution)/shard_map/ppermute | solution.py:57
  203.4 0.7 bitcast_dynamic-update-slice_fusion.4
  204.1 0.7 bitcast_dynamic-update-slice_fusion.3
  204.9 2.6 %collective-permute-done.4 = bf16[1,2,64,1024]{3,2,1,0:T(8,128)(2,1)S(1)} collective-permute-done((bf16[1,2,64,1024]{3,2,1,0:T(8,128)(2,1)S(1)}, bf16[1,2,64,1024]{3,2,1,0:T(8,128)(2,1)S(1)}, u32[]{:S(2)}, u32[]{:S(2)}) %collective-permute-start.4) | collective-permute-done | bytes 262176 | tf_op jit(solution)/shard_map/ppermute | solution.py:57
  207.5 0.7 bitcast_dynamic-update-slice_fusion.2
  208.2 17.9 %collective-permute-done.5 = bf16[1,2,64,1024]{3,2,1,0:T(8,128)(2,1)S(1)} collective-permute-done((bf16[1,2,64,1024]{3,2,1,0:T(8,128)(2,1)S(1)}, bf16[1,2,64,1024]{3,2,1,0:T(8,128)(2,1)S(1)}, u32[]{:S(2)}, u32[]{:S(2)}) %collective-permute-start.5) | collective-permute-done | bytes 262176 | tf_op jit(solution)/shard_map/ppermute | solution.py:57
  226.2 0.7 bitcast_dynamic-update-slice_fusion.1
  226.9 5.2 %collective-permute-done.6 = bf16[1,2,64,1024]{3,2,0,1:T(8,128)(2,1)S(1)} collective-permute-done((bf16[1,2,64,1024]{3,2,0,1:T(8,128)(2,1)S(1)}, bf16[1,2,64,1024]{3,2,0,1:T(8,128)(2,1)S(1)}, u32[]{:S(2)}, u32[]{:S(2)}) %collective-permute-start.6) | collective-permute-done | bytes 262176 | tf_op jit(solution)/shard_map/ppermute | solution.py:57
  232.1 0.7 bitcast_dynamic-update-slice_fusion
  232.8 3.6 %gather_fusion = bf16[8,2,64,1024]{3,2,1,0:T(8,128)(2,1)} fusion(bf16[8,2,64,1024]{3,2,1,0:T(8,128)(2,1)} %bitcast.19, s32[1024]{0:T(1024)S(1)} %pad_clamp_fusion), kind=kCustom, calls=%fused_computation | custom fusion | bytes 4194336 | tf_op jit(solution)/shard_map/gather | solution.py:58
  236.4 2.2 fusion.24
  238.6 1.1 fusion.20
  (29 shorter events, 2.5 us)
Async XLA Ops:
  6.5 107.8 %copy-start = (bf16[2,384,2048]{2,1,0:T(8,128)(2,1)S(1)}, bf16[2,384,2048]{2,1,0:T(8,128)(2,1)}, u32[]{:S(2)}) copy-start(bf16[2,384,2048]{2,1,0:T(8,128)(2,1)} %param.11) | copy-start | bytes 9437188
  6.5 172.5 %reduce-scatter.2.cloned.1.call-start = ((), (), s32[]{:S(2)}) async-start(), calls=%async_computation.2 | async-start | bytes 6291456 | tf_op jit(solution)/shard_map/reduce_scatter | solution.py:49
  13.0 97.7 %copy-start.4 = (bf16[2,2048,384]{2,1,0:T(8,128)(2,1)S(1)}, bf16[2,2048,384]{2,1,0:T(8,128)(2,1)}, u32[]{:S(2)}) copy-start(bf16[2,2048,384]{2,1,0:T(8,128)(2,1)} %param.9) | copy-start | bytes 9437188
  108.8 2.0 copy-start.2
  122.6 0.7 copy-start.3
  180.6 7.6 %collective-permute-start = (bf16[1,2,64,1024]{3,2,1,0:T(8,128)(2,1)S(1)}, bf16[1,2,64,1024]{3,2,1,0:T(8,128)(2,1)S(1)}, u32[]{:S(2)}, u32[]{:S(2)}) collective-permute-start(bf16[1,2,64,1024]{3,2,1,0:T(8,128)(2,1)S(1)} %get-tuple-element.10), channel_id=1, source_target_pairs={{0,2},{2,0},{4,6},{6,4},{8,10},{10,8},{12,14},{14,12},{1,3},{3,1},... | collective-permute-start | bytes 786440 | tf_op jit(solution)/shard_map/ppermute | solution.py:57
  182.1 15.7 %collective-permute-start.1 = (bf16[1,2,64,1024]{3,2,1,0:T(8,128)(2,1)S(1)}, bf16[1,2,64,1024]{3,2,1,0:T(8,128)(2,1)S(1)}, u32[]{:S(2)}, u32[]{:S(2)}) collective-permute-start(bf16[1,2,64,1024]{3,2,1,0:T(8,128)(2,1)S(1)} %get-tuple-element.9), channel_id=1, source_target_pairs={{0,4},{2,6},{4,0},{6,2},{8,12},{10,14},{12,8},{14,10},{1,5},{3,7},... | collective-permute-start | bytes 786440 | tf_op jit(solution)/shard_map/ppermute | solution.py:57
  183.3 20.1 %collective-permute-start.2 = (bf16[1,2,64,1024]{3,2,1,0:T(8,128)(2,1)S(1)}, bf16[1,2,64,1024]{3,2,1,0:T(8,128)(2,1)S(1)}, u32[]{:S(2)}, u32[]{:S(2)}) collective-permute-start(bf16[1,2,64,1024]{3,2,1,0:T(8,128)(2,1)S(1)} %get-tuple-element.8), channel_id=1, source_target_pairs={{0,6},{2,4},{4,2},{6,0},{8,14},{10,12},{12,10},{14,8},{1,7},{3,5},... | collective-permute-start | bytes 786440 | tf_op jit(solution)/shard_map/ppermute | solution.py:57
  183.8 20.3 %collective-permute-start.3 = (bf16[1,2,64,1024]{3,2,1,0:T(8,128)(2,1)S(1)}, bf16[1,2,64,1024]{3,2,1,0:T(8,128)(2,1)S(1)}, u32[]{:S(2)}, u32[]{:S(2)}) collective-permute-start(bf16[1,2,64,1024]{3,2,1,0:T(8,128)(2,1)S(1)} %get-tuple-element.7), channel_id=1, source_target_pairs={{0,8},{2,10},{4,12},{6,14},{8,0},{10,2},{12,4},{14,6},{1,9},{3,11}... | collective-permute-start | bytes 786440 | tf_op jit(solution)/shard_map/ppermute | solution.py:57
  184.0 23.5 %collective-permute-start.4 = (bf16[1,2,64,1024]{3,2,1,0:T(8,128)(2,1)S(1)}, bf16[1,2,64,1024]{3,2,1,0:T(8,128)(2,1)S(1)}, u32[]{:S(2)}, u32[]{:S(2)}) collective-permute-start(bf16[1,2,64,1024]{3,2,1,0:T(8,128)(2,1)S(1)} %get-tuple-element.6), channel_id=1, source_target_pairs={{0,10},{2,8},{4,14},{6,12},{8,2},{10,0},{12,6},{14,4},{1,11},{3,9}... | collective-permute-start | bytes 786440 | tf_op jit(solution)/shard_map/ppermute | solution.py:57
  188.2 38.0 %collective-permute-start.5 = (bf16[1,2,64,1024]{3,2,1,0:T(8,128)(2,1)S(1)}, bf16[1,2,64,1024]{3,2,1,0:T(8,128)(2,1)S(1)}, u32[]{:S(2)}, u32[]{:S(2)}) collective-permute-start(bf16[1,2,64,1024]{3,2,1,0:T(8,128)(2,1)S(1)} %get-tuple-element.11), channel_id=1, source_target_pairs={{0,12},{2,14},{4,8},{6,10},{8,4},{10,6},{12,0},{14,2},{1,13},{3,15... | collective-permute-start | bytes 786440 | tf_op jit(solution)/shard_map/ppermute | solution.py:57
  197.8 34.3 %collective-permute-start.6 = (bf16[1,2,64,1024]{3,2,0,1:T(8,128)(2,1)S(1)}, bf16[1,2,64,1024]{3,2,0,1:T(8,128)(2,1)S(1)}, u32[]{:S(2)}, u32[]{:S(2)}) collective-permute-start(bf16[1,2,64,1024]{3,2,0,1:T(8,128)(2,1)S(1)} %get-tuple-element.5), channel_id=1, source_target_pairs={{0,14},{2,12},{4,10},{6,8},{8,6},{10,4},{12,2},{14,0},{1,15},{3,13... | collective-permute-start | bytes 786440 | tf_op jit(solution)/shard_map/ppermute | solution.py:57
  236.4 2.2 copy-start.1
Sparse Core Ops, SparseCore 0:
  122.7 56.2 reduce-scatter.1
